TPU v7x, 128 devices: a whole 4x4x4 slice. The times are simulated.
128 devices in a mesh: row: 8 (over z, x_lo), col: 16 (over y, x_hi, core).
Axes of the slice: x: 4 (x_hi: 2, x_lo: 2; x = x_hi * 2 + x_lo), y: 4, z: 4, core: 2. Of those that a mesh axis runs over, the one named last changes fastest.
Arguments:
- q_halves: float32 [2, 5120, 5120], P(None, 'row', 'col'), may hold values from -6 to 6
- pole_values: float32 [10240], replicated, may hold values from -10240 to 10240, as said below
- weights: float32 [10240], replicated, may hold values from -6 to 6
- secular_roots: float32 [10240], replicated, may hold values from -10240 to 20480, as said below
- column_order: int32 [10240], replicated, may hold values from 0 to 10239, each once
- deflated: int32 [10240], replicated, may hold values 0 or 1
- reflectors: float32 [2, 2, 5120, 256], P(None, None, 'row'), may hold values from -0.0625 to 0.0625
- triangles: float32 [2, 256, 256], replicated, may hold values from -1.5 to 1.5
Outputs:
- eigvecs: float32 [2, 5120, 10240], P(None, 'row', 'col')
Inputs may be any that keep to these rules, and one draw needn't show every extreme that they name: `pole_values`: all distinct; sorted, neighbouring poles differ by 0.5 to 1.5. The order of the entries is not sorted. secular_roots[j] lies above pole_values[j], at a quarter to three quarters of the distance to the next larger pole (for the largest pole, of a distance of 0.5 to 1.5), so every pole differs from every root by an eighth or more.
All inputs are finite; a program needn't handle non-finite values.
Results may differ from a plain program's by a relative error of at most 0.00015.
Values sent between devices are 32-bit elements; how exact they have to be, the bound alone decides.
A program may use at most 128 MiB of HBM per device.

v0:
```python
import jax
import jax.numpy as jnp
from jax import lax
from jax.sharding import PartitionSpec as P

EPSILON = 1e-06


def column_scale(zeds, pole_values, chosen_roots):
    ratio = zeds[:, None] / (pole_values[:, None] - chosen_roots[None, :])
    return lax.rsqrt(jnp.sum(ratio * ratio, axis=0) + EPSILON)


def cauchy_tile(zeds, pole_values, secular_roots, deflated, first_row, row_count, source, scale):
    pole_slice = lax.dynamic_slice_in_dim(pole_values, first_row, row_count)
    zed_slice = lax.dynamic_slice_in_dim(zeds, first_row, row_count)
    chosen = jnp.take(secular_roots, source)
    cauchy = zed_slice[:, None] / (pole_slice[:, None] - chosen[None, :]) * scale[None, :]
    row_ids = first_row + jnp.arange(row_count, dtype=jnp.int32)
    unit = (row_ids[:, None] == source[None, :]).astype(jnp.float32)
    return jnp.where(jnp.take(deflated, source)[None, :] > 0, unit, cauchy)


def project(vectors, field):
    return jnp.einsum("hrb,hrc->bc", vectors, field, precision=lax.Precision.HIGHEST)


def expand(vectors, coef):
    return jnp.einsum("hrb,bc->hrc", vectors, coef, precision=lax.Precision.HIGHEST)


def local(
    q_halves, pole_values, weights, secular_roots, column_order, deflated, reflectors, triangles
):
    col_count = lax.axis_size("col")
    half = q_halves.shape[2] * col_count
    width = 2 * half // col_count
    zeds = weights * (1 - deflated).astype(jnp.float32)
    own_cols = lax.axis_index("col") * width + jnp.arange(width, dtype=jnp.int32)
    own_source = jnp.take(column_order, own_cols)
    own_scale = column_scale(zeds, pole_values, jnp.take(secular_roots, own_source))
    piece = lax.all_gather(q_halves, "col", axis=2, tiled=True)
    start = jnp.int32(0)
    count = piece.shape[2]
    mixed = jnp.stack(
        [
            jnp.dot(
                piece[which],
                cauchy_tile(
                    zeds,
                    pole_values,
                    secular_roots,
                    deflated,
                    which * half + start,
                    count,
                    own_source,
                    own_scale,
                ),
                precision=lax.Precision.HIGHEST,
            )
            for which in range(2)
        ]
    )
    upper = jnp.triu(triangles)
    first_raw, second_proj, crossed = lax.psum(
        (
            project(reflectors[0], mixed),
            project(reflectors[1], mixed),
            jnp.einsum(
                "hrb,hrd->bd", reflectors[0], reflectors[1], precision=lax.Precision.HIGHEST
            ),
        ),
        "row",
    )
    second_coef = jnp.dot(upper[1], second_proj, precision=lax.Precision.HIGHEST)
    first_coef = jnp.dot(
        upper[0],
        first_raw - jnp.dot(crossed, second_coef, precision=lax.Precision.HIGHEST),
        precision=lax.Precision.HIGHEST,
    )
    return mixed - expand(reflectors[1], second_coef) - expand(reflectors[0], first_coef)


def solution(mesh):
    placed = (P(None, "row", "col"), P(), P(), P(), P(), P(), P(None, None, "row", None), P())
    return jax.shard_map(
        local, mesh=mesh, in_specs=placed, out_specs=P(None, "row", "col"), check_vma=False
    )
```

profile of v0, /device:TPU:1, one launch (start us, length us, event | category | flops | bytes accessed | tf_op | source)
XLA Modules:
  0.0 433.6 jit_solution(5936565044133273526)
XLA Ops:
  6.5 0.0 all-gather.2.cloned.1.call-start
  6.5 0.7 all-gather.2.cloned.1.call-update
  7.3 0.0 all-reduce.3.cloned.1.call-start
  7.3 0.0 copy-start.3
  7.4 3.9 gather_fusion
  11.3 0.0 copy-done.2
  11.3 0.0 copy-start.4
  11.3 3.9 gather_fusion.1
  15.2 0.0 copy-start.12
  15.2 0.0 copy-start.11
  15.2 3.9 gather_fusion.2
  19.1 3.0 fusion.48
  22.1 5.8 %multiply_reduce_fusion = f32[640]{0:T(1024)S(1)} fusion(f32[640]{0:T(1024)S(1)} %broadcast_select_fusion.1, f32[10240]{0:T(1024)S(1)} %copy-done.11, f32[10240]{0:T(1024)S(1)} %convert_multiply_fusion), kind=kLoop, calls=%fused_computation.3 | loop fusion | flops 26213760 | bytes 87040 | tf_op jit(solution)/shard_map/reduce_sum | solution.py:11
  28.0 137.9 %all-gather.2.cloned.1.call-done = f32[2,640,5120]{1,2,0:T(8,128)} async-done(((f32[2,640,320]{1,2,0:T(8,128)}), f32[2,640,5120]{1,2,0:T(8,128)}) %all-gather.2.cloned.1.call-update) | async-done | bytes 26214416 | tf_op jit(solution)/shard_map/all_gather | solution.py:42
  165.8 10.3 %slice_bitcast_fusion.18 = f32[640,5120]{0,1:T(8,128)} fusion(f32[2,640,5120]{1,2,0:T(8,128)} %all-gather.2.cloned.1.call-done), kind=kLoop, calls=%fused_computation.6.clone.clone.clone.clone.2 | loop fusion | bytes 26214400 | tf_op jit(solution)/shard_map/dot_general | solution.py:47
  176.1 87.6 %fusion.28 = f32[1,640,640]{1,2,0:T(8,128)} fusion(f32[640]{0:T(1024)S(1)} %add_rsqrt_fusion, f32[640]{0:T(1024)S(1)} %broadcast_select_fusion.1, f32[5120]{0:T(1024)S(1)} %get-tuple-element.19, f32[5120]{0:T(1024)S(1)} %get-tuple-element.14, s32[640]{0:T(1024)S(1)} %get-tuple-element.13, pred[640]{0:T(1024)(128)(4,1)S(1)} %get-tuple-element.10, ...), kind=kOutput, calls=%fused_computation.38 | convolution fusion | flops 25185484800 | bytes 14794880 | tf_op jit(solution)/shard_map/dot_general | solution.py:47
  263.6 10.3 %slice_bitcast_fusion.19 = f32[640,5120]{0,1:T(8,128)} fusion(f32[2,640,5120]{1,2,0:T(8,128)} %all-gather.2.cloned.1.call-done), kind=kLoop, calls=%fused_computation.4.clone.clone.clone.clone.2 | loop fusion | bytes 26214400 | tf_op jit(solution)/shard_map/dot_general | solution.py:47
  273.9 41.2 %fusion.31 = f32[1,640,640]{1,2,0:T(8,128)S(1)} fusion(f32[5120]{0:T(1024)S(1)} %get-tuple-element.18, f32[5120]{0:T(1024)S(1)} %get-tuple-element.15, f32[640]{0:T(1024)S(1)} %add_rsqrt_fusion, f32[640]{0:T(1024)S(1)} %broadcast_select_fusion.1, s32[640]{0:T(1024)S(1)} %get-tuple-element.13, s32[5120]{0:T(1024)S(1)} %iota_add_fusion, ...), kind=kOutput, calls=%fused_computation.39 | convolution fusion | flops 25185484800 | bytes 14815360 | tf_op jit(solution)/shard_map/dot_general | solution.py:47
  315.1 3.6 fusion.45
  318.7 3.6 fusion.42
  322.3 0.0 all-reduce.3.cloned.1.call-update
  322.3 0.1 iota_compare_fusion.2
  322.4 1.1 broadcast_select_fusion
  323.5 83.7 %all-reduce.3.cloned.1.call-done = (f32[256,640]{0,1:T(8,128)}, f32[256,640]{0,1:T(8,128)}, f32[256,256]{1,0:T(8,128)}) async-done(((f32[256,640]{0,1:T(8,128)}, f32[256,640]{0,1:T(8,128)}, f32[256,256]{1,0:T(8,128)}), (f32[256,640]{0,1:T(8,128)}, f32[256,640]{0,1:T(8,128)}, f32[256,256]{1,0:T(8,128)})) %all-reduce.3.cloned.1.call-update) | async-done | bytes 1572880 | tf_op jit(solution)/shard_map/psum | solution.py:65
  407.2 2.0 fusion.60
  409.2 0.0 copy-start.6
  409.2 5.8 %fusion.39 = f32[640,2,640]{2,0,1:T(8,128)S(1)} fusion(f32[2,2,640,256]{3,2,1,0:T(8,128)S(1)} %copy-done.4, f32[256,640]{1,0:T(8,128)S(1)} %fusion.60), kind=kOutput, calls=%fused_computation.45 | convolution fusion | flops 2516582400 | bytes 5242880 | tf_op jit(solution)/shard_map/hrb,bc->hrc/dot_general | solution.py:29
  415.0 1.2 convolution_subtract_fusion
  416.2 0.7 convolution_bitcast_fusion
  417.0 0.0 copy-start.1
  417.0 5.0 %bitcast_subtract_fusion = f32[2,640,640]{1,2,0:T(8,128)} fusion(f32[640,2,640]{2,0,1:T(8,128)S(1)} %fusion.39, f32[1,640,640]{1,2,0:T(8,128)S(1)} %copy-done.8, f32[1,640,640]{1,2,0:T(8,128)S(1)} %copy-done.6, f32[256,640,1]{0,1,2:T(8,128)S(1)} %convolution_bitcast_fusion, f32[2,2,640,256]{3,2,1,0:T(8,128)S(1)} %copy-done.4), kind=kOutput, calls=%fused_computation.34 | convolution fusion | flops 2519040000 | bytes 11796480 | tf_op jit(solution)/shard_map/hrb,bc->hrc/dot_general | solution.py:29
  422.0 4.6 %copy.17 = f32[2,640,640]{2,1,0:T(8,128)} copy(f32[2,640,640]{1,2,0:T(8,128)} %bitcast_subtract_fusion) | data formatting | bytes 6553600 | tf_op jit(solution)/shard_map/sub | solution.py:81
  (30 shorter events, 0.1 us)
Async XLA Ops:
  6.5 0.8 copy-start
  6.5 4.7 %copy-start.2 = (s32[10240]{0:T(1024)S(1)}, s32[10240]{0:T(1024)}, u32[]{:S(2)}) copy-start(s32[10240]{0:T(1024)} %param.17) | copy-start | bytes 122884
  6.5 159.3 %all-gather.2.cloned.1.call-start = ((), (), s32[]{:S(2)}) async-start(), calls=%async_computation | async-start | bytes 27852800 | tf_op jit(solution)/shard_map/all_gather | solution.py:42
  7.3 400.0 %all-reduce.3.cloned.1.call-start = ((), (), s32[]{:S(2)}) async-start(), calls=%async_computation.1 | async-start | bytes 3145728 | tf_op jit(solution)/shard_map/psum | solution.py:65
  7.3 7.8 %copy-start.3 = (f32[10240]{0:T(1024)S(1)}, f32[10240]{0:T(1024)}, u32[]{:S(2)}) copy-start(f32[10240]{0:T(1024)} %param.15) | copy-start | bytes 122884
  11.3 7.8 %copy-start.4 = (f32[2,2,640,256]{3,2,1,0:T(8,128)S(1)}, f32[2,2,640,256]{3,2,1,0:T(8,128)}, u32[]{:S(2)}) copy-start(f32[2,2,640,256]{3,2,1,0:T(8,128)} %param.18) | copy-start | bytes 7864324
  15.2 6.9 %copy-start.12 = (f32[10240]{0:T(1024)S(1)}, f32[10240]{0:T(1024)}, u32[]{:S(2)}) copy-start(f32[10240]{0:T(1024)} %param.14) | copy-start | bytes 122884
  15.2 7.0 %copy-start.11 = (f32[10240]{0:T(1024)S(1)}, f32[10240]{0:T(1024)}, u32[]{:S(2)}) copy-start(f32[10240]{0:T(1024)} %param.13) | copy-start | bytes 122884
  273.9 41.2 %copy-start.5 = (f32[1,640,640]{1,2,0:T(8,128)S(1)}, f32[1,640,640]{1,2,0:T(8,128)}, u32[]{:S(2)}) copy-start(f32[1,640,640]{1,2,0:T(8,128)} %fusion.28) | copy-start | bytes 4915204
  315.1 3.6 copy-start.7
  407.2 7.8 %copy-start.9 = (f32[256,640]{0,1:T(8,128)S(1)}, f32[256,640]{0,1:T(8,128)}, u32[]{:S(2)}) copy-start(f32[256,640]{0,1:T(8,128)} %get-tuple-element.8) | copy-start | bytes 1966084
  407.2 7.8 %copy-start.10 = (f32[256,256]{1,0:T(8,128)S(1)}, f32[256,256]{1,0:T(8,128)}, u32[]{:S(2)}) copy-start(f32[256,256]{1,0:T(8,128)} %get-tuple-element.9) | copy-start | bytes 786436
  409.2 7.8 %copy-start.6 = (f32[1,640,640]{1,2,0:T(8,128)S(1)}, f32[1,640,640]{1,2,0:T(8,128)}, u32[]{:S(2)}) copy-start(f32[1,640,640]{1,2,0:T(8,128)} %fusion.28) | copy-start | bytes 4915204
  409.2 7.8 %copy-start.8 = (f32[1,640,640]{1,2,0:T(8,128)S(1)}, f32[1,640,640]{1,2,0:T(8,128)}, u32[]{:S(2)}) copy-start(f32[1,640,640]{1,2,0:T(8,128)} %copy-done.7) | copy-start | bytes 4915204
  417.0 9.5 %copy-start.1 = (s32[10240]{0:T(1024)S(1)}, s32[10240]{0:T(1024)}, u32[]{:S(2)}) copy-start(s32[10240]{0:T(1024)} %param.16) | copy-start | bytes 122884
Sparse Core Ops, SparseCore 0:
  9.8 155.9 all-gather.1
  322.4 84.7 all-reduce.2
where the time goes:
time: 438 us; the launch traced here: 434 us
  waiting for transfers between devices  222 us (51%)
  matrix products  154 us (35%)
  local copies, waits for them, and re-layouts  36.7 us (8%)
  between operations  13.9 us (3%)
  other arithmetic  7.06 us (2%)
    all_gather x1, waiting for transfers between devices, local(): piece = lax.all_gather(q_halves, 'col', axis=2, tiled=True)  138 us
    dot_general x2, matrix products, local(): jnp.dot(piece[which], cauchy_tile(zeds, pole_values, secular_roots, defla...  129 us
    psum x1, waiting for transfers between devices, local(): lax.psum((project(reflectors[0], mixed), project(reflectors[1], mixed), j...  83.7 us
    dot_general x2, local copies, waits for them, and re-layouts, local(): jnp.dot(piece[which], cauchy_tile(zeds, pole_values, secular_roots, defla...  20.5 us
    dot_general x2, matrix products, expand(): jnp.einsum('hrb,bc->hrc', vectors, coef, precision=lax.Precision.HIGHEST)  10.7 us
  transfers between devices with their start and end apart: 2, of which 2 were waited for; matrix products, arithmetic and copies ran while one was open for 5% of the time, Pallas kernels for 0%

commit v1 on v0

v1 whole, which is shorter than its diff:
```python
import functools

import jax
import jax.numpy as jnp
from jax import lax
from jax.experimental import pallas as pl
from jax.experimental.pallas import tpu as pltpu
from jax.sharding import PartitionSpec as P

EPSILON = 1e-06
MESH = pl.DeviceIdType.MESH
F32 = jnp.float32
BF16 = jnp.bfloat16
TILE = 320
STRIP = 64


def split(value):
    high = value.astype(BF16)
    return high, (value - high.astype(F32)).astype(BF16)


def dot3(a, b, contract):
    dims = (((contract[0],), (contract[1],)), ((), ()))
    one = functools.partial(lax.dot_general, dimension_numbers=dims, preferred_element_type=F32)
    return one(a[0], b[0]) + one(a[0], b[1]) + one(a[1], b[0])


def merge_kernel(
    q_ref, vec_ref, source_ref, roots_ref, poles_ref, weights_ref, deflated_ref, tri_ref,
    mixed_ref, high_ref, low_ref,
    panel, acc, turned, lam, dfl, squares, c_high, c_low, q_high, q_low,
    proj, proj_in, coef, cross, cross_in, cross_all,
    local_sem, send, recv, row_send, row_recv,
):
    r, col = lax.axis_index("row"), lax.axis_index("col")
    y, x, c = col // 4, lax.rem(col // 2, 2), lax.rem(col, 2)
    width = acc.shape[1]
    piece = width // 8

    def dev(dy, dx, dc):
        return (r, lax.rem(y + dy, 4) * 4 + lax.rem(x + dx, 2) * 2 + lax.rem(c + dc, 2))

    def slot(dy, dx):
        return lax.rem(y + dy, 4) * 2 + lax.rem(x + dx, 2)

    up, down, over, twin = dev(1, 0, 0), dev(3, 0, 0), dev(0, 1, 0), dev(0, 0, 1)
    rows = [(lax.rem(r + d, 8), col) for d in range(1, 8)]

    barrier = pltpu.get_barrier_semaphore()
    for other in [up, down, over, twin, *rows]:
        pl.semaphore_signal(barrier, inc=1, device_id=other, device_id_type=MESH)
    pl.semaphore_wait(barrier, 11)

    started = {}

    def ship(name, src, dst, to):
        at = len(started)
        copy = pltpu.make_async_remote_copy(
            src_ref=src, dst_ref=dst, send_sem=send.at[at], recv_sem=recv.at[at],
            device_id=to, device_id_type=MESH,
        )
        copy.start()
        started[name] = copy

    def relay(name, dy, dx, half, to):
        place = panel.at[slot(dy, dx), half, c]
        ship(name, place, place, to)

    own = []
    for half in range(2):
        place = panel.at[slot(0, 0), half, c]
        ship(("up", half), q_ref.at[half], place, up)
        ship(("down", half), q_ref.at[half], place, down)
        ship(("over", half), q_ref.at[half], place, over)
        ship(("twin", 0, 0, half), q_ref.at[half], place, twin)
        mine = pltpu.make_async_copy(q_ref.at[half], place, local_sem.at[half])
        mine.start()
        own.append(mine)

    total = jnp.zeros(cross.shape, F32)
    for half in range(2):
        total += dot3(split(vec_ref[0, half]), split(vec_ref[1, half]), (0, 0))
    cross[...] = total
    small = cross.shape[0] // 8

    def row_copies(base, src_of, dst):
        copies = []
        for d in range(1, 8):
            to = lax.rem(r + d, 8)
            copy = pltpu.make_async_remote_copy(
                src_ref=src_of(to), dst_ref=dst, send_sem=row_send.at[base + d], recv_sem=row_recv.at[base + d],
                device_id=(to, col), device_id_type=MESH,
            )
            copy.start()
            copies.append(copy)
        return copies

    cross_copies = row_copies(0, lambda to: cross.at[pl.ds(to * small, small)], cross_in.at[r])

    lam[...] = jnp.zeros(lam.shape, F32)
    dfl[...] = jnp.zeros(dfl.shape, F32)
    squares[...] = jnp.zeros(squares.shape, F32)
    span = poles_ref.shape[1]

    def find(step, carry):
        at = step * span + lax.broadcasted_iota(jnp.int32, (1, span), 1)
        root = roots_ref[pl.ds(step, 1), :]
        flag = deflated_ref[pl.ds(step, 1), :].astype(F32)

        def strip(i, inner):
            o = pl.ds(pl.multiple_of(i * STRIP, STRIP), STRIP)
            same = source_ref[o, :] == at
            lam[o, :] += jnp.sum(jnp.where(same, root, 0.0), axis=1, keepdims=True)
            dfl[o, :] += jnp.sum(jnp.where(same, flag, 0.0), axis=1, keepdims=True)
            return inner

        return lax.fori_loop(0, width // STRIP, strip, carry)

    lax.fori_loop(0, 2 * panel.shape[0], find, 0)
    acc[...] = jnp.zeros(acc.shape, F32)

    def unit(m, half):
        line = half * 8 + m
        pole = poles_ref[pl.ds(line, 1), :]
        zed = weights_ref[pl.ds(line, 1), :] * (1 - deflated_ref[pl.ds(line, 1), :]).astype(F32)
        at = line * span + lax.broadcasted_iota(jnp.int32, (1, span), 1)
        q_high[...], q_low[...] = split(panel[m, half].reshape(span, width))

        def tile(t, carry):
            def strip(i, inner):
                o = pl.ds(pl.multiple_of(t * TILE + i * STRIP, STRIP), STRIP)
                value = zed / (pole - lam[o, :])
                squares[o, :] += jnp.sum(value * value, axis=1, keepdims=True)
                single = jnp.where(source_ref[o, :] == at, 1.0, 0.0)
                value = jnp.where(dfl[o, :] > 0, single, value)
                into = pl.ds(pl.multiple_of(i * STRIP, STRIP), STRIP)
                c_high[into, :], c_low[into, :] = split(value)
                return inner

            lax.fori_loop(0, TILE // STRIP, strip, 0)
            o = pl.ds(pl.multiple_of(t * TILE, TILE), TILE)
            acc[half, o, :] += dot3((c_high[...], c_low[...]), (q_high[...], q_low[...]), (1, 0))
            return carry

        lax.fori_loop(0, width // TILE, tile, 0)

    def both(step, carry):
        unit(slot(0, 0), step)
        return carry

    for half in range(2):
        own[half].wait()
        started["twin", 0, 0, half].wait_recv()
    lax.fori_loop(0, 2, both, 0)

    for copy in cross_copies:
        copy.wait()
    mine = pl.ds(r * small, small)
    total = cross[mine, :]
    for d in range(1, 8):
        total += cross_in[lax.rem(r + d, 8)]
    cross_all[mine, :] = total
    cross_copies = row_copies(8, lambda to: cross_all.at[mine], cross_all.at[mine])

    def arrive(name, dy, dx, half):
        started[name].wait_recv()
        relay(("twin", dy, dx, half), dy, dx, half, twin)

    def three(half):
        for dy, dx in ((3, 0), (1, 0), (0, 1)):
            started["twin", dy, dx, half].wait_recv()

        def one(i, carry):
            dx = i // 2
            unit(slot(3 - 2 * i + dx, dx), half)
            return carry

        lax.fori_loop(0, 3, one, 0)

    arrive(("up", 0), 3, 0, 0)
    relay(("up2", 0), 3, 0, 0, up)
    arrive(("over", 0), 0, 1, 0)
    relay(("upx", 0), 0, 1, 0, up)
    relay(("downx", 0), 0, 1, 0, down)
    arrive(("down", 0), 1, 0, 0)
    arrive(("down", 1), 1, 0, 1)
    relay(("down2", 1), 1, 0, 1, down)
    arrive(("over", 1), 0, 1, 1)
    relay(("upx", 1), 0, 1, 1, up)
    relay(("downx", 1), 0, 1, 1, down)
    arrive(("up", 1), 3, 0, 1)
    three(0)
    arrive(("up2", 0), 2, 0, 0)
    relay(("over2", 0), 2, 0, 0, over)
    three(1)
    arrive(("down2", 1), 2, 0, 1)
    relay(("over2", 1), 2, 0, 1, over)

    def pair(dys, dx, halves):
        for dy in dys:
            for half in halves:
                started["twin", dy, dx, half].wait_recv()

        def one(i, carry):
            dy = dys[0] + i * (dys[-1] - dys[0])
            unit(slot(dy, dx), halves[0] + i * (halves[-1] - halves[0]))
            return carry

        lax.fori_loop(0, len(dys) * len(halves), one, 0)

    pair((2,), 0, (0, 1))
    for half in range(2):
        arrive(("upx", half), 3, 1, half)
        arrive(("downx", half), 1, 1, half)
        pair((1, 3), 1, (half,))
    arrive(("over2", 0), 2, 1, 0)
    arrive(("over2", 1), 2, 1, 1)
    pair((2,), 1, (0, 1))

    size = vec_ref.shape[3]
    factor = jnp.where(dfl[...] > 0, 1.0, lax.rsqrt(squares[...] + EPSILON))
    lam[...] = factor

    def project(t, carry):
        o = pl.ds(pl.multiple_of(t * TILE, TILE), TILE)
        got = []
        for half in range(2):
            value = acc[half, o, :] * lam[o, :]
            acc[half, o, :] = value
            got.append(split(value))
        for block in range(2):
            proj[o, block * size : (block + 1) * size] = dot3(
                got[0], split(vec_ref[block, 0]), (1, 0)
            ) + dot3(got[1], split(vec_ref[block, 1]), (1, 0))
        return carry

    lax.fori_loop(0, width // TILE, project, 0)
    proj_copies = row_copies(16, lambda to: proj.at[pl.ds(to * piece, piece)], proj_in.at[r])

    for half in range(2):
        turned[half] = acc[half].T
    out = pltpu.make_async_copy(turned, mixed_ref, local_sem.at[2])
    out.start()

    for copy in cross_copies:
        copy.wait()
    for copy in proj_copies:
        copy.wait()
    mine = pl.ds(r * piece, piece)
    total = proj[mine, :]
    for d in range(1, 8):
        total += proj_in[lax.rem(r + d, 8)]
    order = [lax.broadcasted_iota(jnp.int32, (size, size), i) for i in range(2)]
    upper = [split(jnp.where(order[0] <= order[1], tri_ref[i], 0.0)) for i in range(2)]
    second = dot3(split(total[:, size:]), upper[1], (1, 1))
    rest = total[:, :size] - dot3(split(second), split(cross_all[...]), (1, 1))
    coef[mine, :size] = dot3(split(rest), upper[0], (1, 1))
    coef[mine, size:] = second
    for copy in row_copies(24, lambda to: coef.at[mine], coef.at[mine]):
        copy.wait()
    high_ref[...], low_ref[...] = split(coef[...])
    for copy in started.values():
        copy.wait_send()
    out.wait()


def merge(q_turned, vectors, source, roots, poles, weights, deflated, triangles):
    depth, width = q_turned.shape[1], q_turned.shape[2]
    size = vectors.shape[3]
    vmem = pl.BlockSpec(memory_space=pltpu.VMEM)
    hbm = pl.BlockSpec(memory_space=pl.ANY)
    dma = pltpu.SemaphoreType.DMA
    span = 2 * depth
    return pl.pallas_call(
        merge_kernel,
        out_shape=(
            jax.ShapeDtypeStruct((2, width, width), F32),
            jax.ShapeDtypeStruct((width, 2 * size), BF16),
            jax.ShapeDtypeStruct((width, 2 * size), BF16),
        ),
        in_specs=[hbm] + [vmem] * 7,
        out_specs=(hbm, vmem, vmem),
        scratch_shapes=[
            pltpu.VMEM((8, 2, 2, depth, width), F32),
            pltpu.VMEM((2, width, width), F32),
            pltpu.VMEM((2, width, width), F32),
            pltpu.VMEM((width, 1), F32),
            pltpu.VMEM((width, 1), F32),
            pltpu.VMEM((width, 1), F32),
            pltpu.VMEM((TILE, span), BF16),
            pltpu.VMEM((TILE, span), BF16),
            pltpu.VMEM((span, width), BF16),
            pltpu.VMEM((span, width), BF16),
            pltpu.VMEM((width, 2 * size), F32),
            pltpu.VMEM((8, width // 8, 2 * size), F32),
            pltpu.VMEM((width, 2 * size), F32),
            pltpu.VMEM((size, size), F32),
            pltpu.VMEM((8, size // 8, size), F32),
            pltpu.VMEM((size, size), F32),
            dma((3,)),
            dma((32,)),
            dma((32,)),
            dma((32,)),
            dma((32,)),
        ],
        compiler_params=pltpu.CompilerParams(
            collective_id=0, has_side_effects=True, vmem_limit_bytes=60 * 1024 * 1024
        ),
        name="merge",
    )(q_turned, vectors, source, roots, poles, weights, deflated, triangles)


def update_kernel(mixed_ref, vec_ref, high_ref, low_ref, out_ref):
    size = vec_ref.shape[3]
    total = mixed_ref[0]
    for block in range(2):
        take = slice(block * size, (block + 1) * size)
        total -= dot3(split(vec_ref[block, 0]), (high_ref[:, take], low_ref[:, take]), (1, 1))
    out_ref[0] = total


def update(mixed, vectors, high, low):
    _, height, width = mixed.shape
    size = vectors.shape[3]
    part = 320
    whole = pl.BlockSpec((width, 2 * size), lambda h, i: (0, 0))
    return pl.pallas_call(
        update_kernel,
        grid=(2, height // part),
        out_shape=jax.ShapeDtypeStruct(mixed.shape, F32),
        in_specs=[
            pl.BlockSpec((1, part, width), lambda h, i: (h, i, 0)),
            pl.BlockSpec((2, 1, part, size), lambda h, i: (0, h, i, 0)),
            whole,
            whole,
        ],
        out_specs=pl.BlockSpec((1, part, width), lambda h, i: (h, i, 0)),
        compiler_params=pltpu.CompilerParams(vmem_limit_bytes=32 * 1024 * 1024),
        name="update",
    )(mixed, vectors, high, low)


def local(
    q_halves, pole_values, weights, secular_roots, column_order, deflated, reflectors, triangles
):
    depth = q_halves.shape[2]
    col = lax.axis_index("col")
    source = lax.dynamic_slice_in_dim(column_order, col * 2 * depth, 2 * depth).reshape(-1, 1)
    lines = (16, 2 * depth)
    mixed, high, low = merge(
        jnp.swapaxes(q_halves, 1, 2),
        reflectors,
        source,
        secular_roots.reshape(lines),
        pole_values.reshape(lines),
        weights.reshape(lines),
        deflated.reshape(lines),
        triangles,
    )
    return update(mixed, reflectors, high, low)


def solution(mesh):
    placed = (P(None, "row", "col"), P(), P(), P(), P(), P(), P(None, None, "row", None), P())
    return jax.shard_map(
        local, mesh=mesh, in_specs=placed, out_specs=P(None, "row", "col"), check_vma=False
    )
```

time: 438 us -> 190 us (0.43)
  waiting for transfers between devices: 222 us -> 0 us
  Pallas kernels: 0 us -> 178 us
  matrix products: 154 us -> 0 us
  local copies, waits for them, and re-layouts: 36.7 us -> 11.5 us
  between operations: 13.9 us -> 0.03 us
  other arithmetic: 7.06 us -> 0 us
    pallas_call x0 -> x2, Pallas kernels: none -> 178 us  [the longest x1 173 us: merge(): pl.pallas_call(merge_kernel, out_shape=(jax.ShapeDtypeStruct((2, width, w...]
    dot_general x10 -> x0, matrix products: 154 us -> none  [the longest x2 129 us: local(): jnp.dot(piece[which], cauchy_tile(zeds, pole_values, secular_roots, defla...]
    all_gather x1 -> x0, waiting for transfers between devices: 138 us -> none  [local(): piece = lax.all_gather(q_halves, 'col', axis=2, tiled=True)]
    psum x1 -> x0, waiting for transfers between devices: 83.7 us -> none  [local(): lax.psum((project(reflectors[0], mixed), project(reflectors[1], mixed), j...]
    dot_general x2 -> x0, local copies, waits for them, and re-layouts: 20.5 us -> none  [local(): jnp.dot(piece[which], cauchy_tile(zeds, pole_values, secular_roots, defla...]
    gather x3 -> x0, local copies, waits for them, and re-layouts: 11.6 us -> none  [the longest x1 3.86 us: local(): own_source = jnp.take(column_order, own_cols)]
    reshape x0 -> x5, local copies, waits for them, and re-layouts: none -> 6.48 us  [the longest x1 1.4 us: local(): pole_values.reshape(lines)]
    reduce_sum x1 -> x0, other arithmetic: 5.78 us -> none  [column_scale(): return lax.rsqrt(jnp.sum(ratio * ratio, axis=0) + EPSILON)]
  transfers between devices with their start and end apart: 2 -> 0, of which waited for: 2 -> 0; matrix products, arithmetic and copies ran while one was open for 5% -> 0% of each run, Pallas kernels for 0% -> 0%
where the time goes in v1:
time: 190 us
  Pallas kernels  178 us (94%)
  local copies, waits for them, and re-layouts  11.5 us (6%)
    pallas_call x1, Pallas kernels, merge(): pl.pallas_call(merge_kernel, out_shape=(jax.ShapeDtypeStruct((2, width, w...  173 us
    pallas_call x1, Pallas kernels, update(): pl.pallas_call(update_kernel, grid=(2, height // part), out_shape=jax.Sha...  5.01 us
    unnamed x8, local copies, waits for them, and re-layouts  4.1 us

profile of v1, /device:TPU:1, one launch (start us, length us, event | category | flops | bytes accessed | tf_op | source)
XLA Modules:
  0.0 189.6 jit_solution(13228486938573420196)
XLA Ops:
  0.0 0.0 copy-start
  0.0 0.9 dynamic_slice.3
  0.9 1.4 reshape.17.poles_ref
  2.3 1.4 reshape.18.weights_ref
  3.7 1.4 reshape.16.roots_ref
  5.1 1.4 reshape.19.deflated_ref
  6.5 0.9 reshape.20.source_ref
  7.4 173.0 %merge.1 = (f32[2,640,640]{2,1,0:T(8,128)}, bf16[640,512]{1,0:T(8,128)(2,1)}, bf16[640,512]{1,0:T(8,128)(2,1)}) custom-call(f32[2,320,640]{2,1,0:T(8,128)} %bitcast.1, f32[2,2,640,256]{3,2,1,0:T(8,128)} %vec_ref.3, s32[640,1]{1,0:T(8,128)} %reshape.20.source_ref, f32[16,640]{1,0:T(8,128)} %reshape.16.roots_ref, f32[16,640]{1,0:T(8,128)} %reshape.17.poles_ref, ...), custom_call_target="tpu_custom_call" | custom-call | tf_op jit(solution)/shard_map/merge/pallas_call | solution.py:275
  180.4 0.0 copy-done
  180.4 0.0 copy-start.1
  180.5 1.9 %copy-done.1 = f32[2,640,640]{2,1,0:T(8,128)S(1)} copy-done((f32[2,640,640]{2,1,0:T(8,128)S(1)}, f32[2,640,640]{2,1,0:T(8,128)}, u32[]{:S(2)}) %copy-start.1) | copy-done | bytes 3276824
  182.4 0.0 copy-start.2
  182.4 1.1 copy-done.2
  183.5 0.0 copy-start.3
  183.5 1.1 copy-done.3
  184.5 5.0 %update.1 = f32[2,640,640]{2,1,0:T(8,128)} custom-call(f32[2,640,640]{2,1,0:T(8,128)S(1)} %copy-done.1, f32[2,2,640,256]{3,2,1,0:T(8,128)S(1)} %copy-done, bf16[640,512]{1,0:T(8,128)(2,1)S(1)} %copy-done.2, bf16[640,512]{1,0:T(8,128)(2,1)S(1)} %copy-done.3), custom_call_target="tpu_custom_call" | custom-call | tf_op jit(solution)/shard_map/update/pallas_call | solution.py:328
Async XLA Ops:
  0.0 180.4 %copy-start = (f32[2,2,640,256]{3,2,1,0:T(8,128)S(1)}, f32[2,2,640,256]{3,2,1,0:T(8,128)}, u32[]{:S(2)}) copy-start(f32[2,2,640,256]{3,2,1,0:T(8,128)} %vec_ref.3) | copy-start | bytes 7864324
  180.4 1.9 %copy-start.1 = (f32[2,640,640]{2,1,0:T(8,128)S(1)}, f32[2,640,640]{2,1,0:T(8,128)}, u32[]{:S(2)}) copy-start(f32[2,640,640]{2,1,0:T(8,128)} %get-tuple-element.8.mixed_ref) | copy-start | bytes 9830404
  182.4 1.1 copy-start.2
  183.5 1.1 copy-start.3

commit v2 on v1

--- a/solution.py
+++ b/solution.py
@@ -12,6 +12,7 @@
 F32 = jnp.float32
 BF16 = jnp.bfloat16
 TILE = 320
+LANES = 128
 STRIP = 64
 
 
@@ -27,9 +28,9 @@
 
 
 def merge_kernel(
-    q_ref, vec_ref, source_ref, roots_ref, poles_ref, weights_ref, deflated_ref, tri_ref,
+    q_ref, vec_ref, order_ref, roots_ref, lines_ref, weights_ref, deflated_ref, tri_ref,
     mixed_ref, high_ref, low_ref,
-    panel, acc, turned, lam, dfl, squares, c_high, c_low, q_high, q_low,
+    panel, acc, turned, poles_ref, zeds_ref, source, lam, keep, squares, c_high, c_low, q_high, q_low,
     proj, proj_in, coef, cross, cross_in, cross_all,
     local_sem, send, recv, row_send, row_recv,
 ):
@@ -70,13 +71,13 @@
     own = []
     for half in range(2):
         place = panel.at[slot(0, 0), half, c]
-        ship(("up", half), q_ref.at[half], place, up)
-        ship(("down", half), q_ref.at[half], place, down)
-        ship(("over", half), q_ref.at[half], place, over)
-        ship(("twin", 0, 0, half), q_ref.at[half], place, twin)
         mine = pltpu.make_async_copy(q_ref.at[half], place, local_sem.at[half])
         mine.start()
         own.append(mine)
+        ship(("up", half), q_ref.at[half], place, up)
+        other = panel.at[slot(0, 0), 1 - half, c]
+        ship(("down", 1 - half), q_ref.at[1 - half], other, down)
+        ship(("twin", 0, 0, half), q_ref.at[half], place, twin)
 
     total = jnp.zeros(cross.shape, F32)
     for half in range(2):
@@ -98,61 +99,101 @@
 
     cross_copies = row_copies(0, lambda to: cross.at[pl.ds(to * small, small)], cross_in.at[r])
 
-    lam[...] = jnp.zeros(lam.shape, F32)
-    dfl[...] = jnp.zeros(dfl.shape, F32)
+    for half in range(2):
+        ship(("over", half), q_ref.at[half], panel.at[slot(0, 0), half, c], over)
+
+    span = 2 * panel.shape[3]
+    group = span // LANES
+    for line in range(2 * panel.shape[0]):
+        for i in range(group):
+            at = slice(line * group + i, line * group + i + 1)
+            into = (slice(line, line + 1), slice(i * LANES, (i + 1) * LANES))
+            poles_ref[into] = lines_ref[at, :]
+            zeds_ref[into] = weights_ref[at, :] * (1 - deflated_ref[at, :]).astype(F32)
+
     squares[...] = jnp.zeros(squares.shape, F32)
-    span = poles_ref.shape[1]
-
-    def find(step, carry):
-        at = step * span + lax.broadcasted_iota(jnp.int32, (1, span), 1)
-        root = roots_ref[pl.ds(step, 1), :]
-        flag = deflated_ref[pl.ds(step, 1), :].astype(F32)
-
-        def strip(i, inner):
-            o = pl.ds(pl.multiple_of(i * STRIP, STRIP), STRIP)
-            same = source_ref[o, :] == at
-            lam[o, :] += jnp.sum(jnp.where(same, root, 0.0), axis=1, keepdims=True)
-            dfl[o, :] += jnp.sum(jnp.where(same, flag, 0.0), axis=1, keepdims=True)
-            return inner
-
-        return lax.fori_loop(0, width // STRIP, strip, carry)
-
-    lax.fori_loop(0, 2 * panel.shape[0], find, 0)
     acc[...] = jnp.zeros(acc.shape, F32)
+    for i in range(width // LANES):
+        own_line = order_ref[pl.ds(col * (width // LANES) + i, 1), :].astype(F32)
+        source[i * LANES : (i + 1) * LANES, :] = jnp.broadcast_to(own_line, (LANES, LANES)).T
+
+    def find(i, carry):
+        o = pl.ds(pl.multiple_of(i * STRIP, STRIP), STRIP)
+        wanted = source[o, :].astype(jnp.int32)
+
+        def line(step, found):
+            same = wanted == step * LANES + lax.broadcasted_iota(jnp.int32, (1, LANES), 1)
+            flag = deflated_ref[pl.ds(step, 1), :].astype(F32)
+            return (
+                found[0] + jnp.where(same, roots_ref[pl.ds(step, 1), :], 0.0),
+                found[1] + jnp.where(same, flag, 0.0),
+            )
+
+        zero = jnp.zeros((STRIP, LANES), F32)
+        root, flag = lax.fori_loop(0, roots_ref.shape[0], line, (zero, zero))
+        flag = jnp.sum(flag, axis=1, keepdims=True)
+        lam[o, :] = jnp.broadcast_to(jnp.sum(root, axis=1, keepdims=True), (STRIP, LANES))
+        keep[o, :] = jnp.broadcast_to(1.0 - flag, (STRIP, LANES))
+        source[o, :] = jnp.where(flag > 0, source[o, :], -1.0)
+        return carry
+
+    lax.fori_loop(0, width // STRIP, find, 0)
 
     def unit(m, half):
-        line = half * 8 + m
-        pole = poles_ref[pl.ds(line, 1), :]
-        zed = weights_ref[pl.ds(line, 1), :] * (1 - deflated_ref[pl.ds(line, 1), :]).astype(F32)
-        at = line * span + lax.broadcasted_iota(jnp.int32, (1, span), 1)
+        at = half * 8 + m
+        pole = poles_ref[pl.ds(at, 1), :]
+        zed = zeds_ref[pl.ds(at, 1), :]
+        count = (at * span + lax.broadcasted_iota(jnp.int32, (1, span), 1)).astype(F32)
         q_high[...], q_low[...] = split(panel[m, half].reshape(span, width))
-
-        def tile(t, carry):
-            def strip(i, inner):
-                o = pl.ds(pl.multiple_of(t * TILE + i * STRIP, STRIP), STRIP)
-                value = zed / (pole - lam[o, :])
-                squares[o, :] += jnp.sum(value * value, axis=1, keepdims=True)
-                single = jnp.where(source_ref[o, :] == at, 1.0, 0.0)
-                value = jnp.where(dfl[o, :] > 0, single, value)
-                into = pl.ds(pl.multiple_of(i * STRIP, STRIP), STRIP)
-                c_high[into, :], c_low[into, :] = split(value)
-                return inner
-
-            lax.fori_loop(0, TILE // STRIP, strip, 0)
-            o = pl.ds(pl.multiple_of(t * TILE, TILE), TILE)
-            acc[half, o, :] += dot3((c_high[...], c_low[...]), (q_high[...], q_low[...]), (1, 0))
+        for t in range(width // TILE):
+            for i in range(TILE // STRIP):
+                o = slice(t * TILE + i * STRIP, t * TILE + (i + 1) * STRIP)
+                into = slice(i * STRIP, (i + 1) * STRIP)
+                total = squares[o, :]
+                for k in range(group):
+                    lanes = slice(k * LANES, (k + 1) * LANES)
+                    gap = pole[:, lanes] - lam[o, :]
+                    guess = pl.reciprocal(gap, approx=True)
+                    guess = guess * (2.0 - gap * guess)
+                    value = zed[:, lanes] * guess
+                    total += value * value
+                    value = jnp.where(source[o, :] == count[:, lanes], 1.0, value * keep[o, :])
+                    c_high[t, into, lanes], c_low[t, into, lanes] = split(value)
+                squares[o, :] = total
+        for t in range(width // TILE):
+            o = slice(t * TILE, (t + 1) * TILE)
+            acc[half, o, :] += dot3((c_high[t], c_low[t]), (q_high[...], q_low[...]), (1, 0))
+
+    def run(steps, place):
+        def one(i, carry):
+            dy, dx, half = place(i)
+            unit(slot(dy, dx), half)
             return carry
 
-        lax.fori_loop(0, width // TILE, tile, 0)
-
-    def both(step, carry):
-        unit(slot(0, 0), step)
-        return carry
+        lax.fori_loop(0, steps, one, 0)
+
+    def arrive(name, dy, dx, half):
+        started[name].wait_recv()
+        relay(("twin", dy, dx, half), dy, dx, half, twin)
+
+    def ready(*places):
+        for dy, dx, half in places:
+            started["twin", dy, dx, half].wait_recv()
 
     for half in range(2):
         own[half].wait()
-        started["twin", 0, 0, half].wait_recv()
-    lax.fori_loop(0, 2, both, 0)
+    ready((0, 0, 0), (0, 0, 1))
+    run(2, lambda i: (0, 0, i))
+
+    arrive(("up", 0), 3, 0, 0)
+    relay(("up2", 0), 3, 0, 0, up)
+    arrive(("down", 1), 1, 0, 1)
+    relay(("down2", 1), 1, 0, 1, down)
+    arrive(("over", 0), 0, 1, 0)
+    relay(("upx", 0), 0, 1, 0, up)
+    relay(("downx", 0), 0, 1, 0, down)
+    ready((3, 0, 0), (1, 0, 1), (0, 1, 0))
+    run(3, lambda i: (3 - 2 * i + i // 2, i // 2, lax.rem(i, 2)))
 
     for copy in cross_copies:
         copy.wait()
@@ -163,70 +204,37 @@
     cross_all[mine, :] = total
     cross_copies = row_copies(8, lambda to: cross_all.at[mine], cross_all.at[mine])
 
-    def arrive(name, dy, dx, half):
-        started[name].wait_recv()
-        relay(("twin", dy, dx, half), dy, dx, half, twin)
-
-    def three(half):
-        for dy, dx in ((3, 0), (1, 0), (0, 1)):
-            started["twin", dy, dx, half].wait_recv()
-
-        def one(i, carry):
-            dx = i // 2
-            unit(slot(3 - 2 * i + dx, dx), half)
-            return carry
-
-        lax.fori_loop(0, 3, one, 0)
-
-    arrive(("up", 0), 3, 0, 0)
-    relay(("up2", 0), 3, 0, 0, up)
-    arrive(("over", 0), 0, 1, 0)
-    relay(("upx", 0), 0, 1, 0, up)
-    relay(("downx", 0), 0, 1, 0, down)
+    arrive(("up", 1), 3, 0, 1)
     arrive(("down", 0), 1, 0, 0)
-    arrive(("down", 1), 1, 0, 1)
-    relay(("down2", 1), 1, 0, 1, down)
     arrive(("over", 1), 0, 1, 1)
     relay(("upx", 1), 0, 1, 1, up)
     relay(("downx", 1), 0, 1, 1, down)
-    arrive(("up", 1), 3, 0, 1)
-    three(0)
+    ready((3, 0, 1), (1, 0, 0), (0, 1, 1))
+    run(3, lambda i: (3 - 2 * i + i // 2, i // 2, 1 - lax.rem(i, 2)))
+
     arrive(("up2", 0), 2, 0, 0)
     relay(("over2", 0), 2, 0, 0, over)
-    three(1)
     arrive(("down2", 1), 2, 0, 1)
     relay(("over2", 1), 2, 0, 1, over)
-
-    def pair(dys, dx, halves):
-        for dy in dys:
-            for half in halves:
-                started["twin", dy, dx, half].wait_recv()
-
-        def one(i, carry):
-            dy = dys[0] + i * (dys[-1] - dys[0])
-            unit(slot(dy, dx), halves[0] + i * (halves[-1] - halves[0]))
-            return carry
-
-        lax.fori_loop(0, len(dys) * len(halves), one, 0)
-
-    pair((2,), 0, (0, 1))
+    ready((2, 0, 0), (2, 0, 1))
+    run(2, lambda i: (2, 0, i))
+
     for half in range(2):
         arrive(("upx", half), 3, 1, half)
         arrive(("downx", half), 1, 1, half)
-        pair((1, 3), 1, (half,))
-    arrive(("over2", 0), 2, 1, 0)
-    arrive(("over2", 1), 2, 1, 1)
-    pair((2,), 1, (0, 1))
+        arrive(("over2", half), 2, 1, half)
+        ready((3, 1, half), (1, 1, half), (2, 1, half))
+        run(3, lambda i, half=half: (3 - 2 * i + 3 * (i // 2), 1, half))
 
     size = vec_ref.shape[3]
-    factor = jnp.where(dfl[...] > 0, 1.0, lax.rsqrt(squares[...] + EPSILON))
-    lam[...] = factor
+    norm = lax.rsqrt(jnp.sum(squares[...], axis=1, keepdims=True) + EPSILON)
+    lam[...] = jnp.where(keep[...] > 0, norm, 1.0)
 
     def project(t, carry):
         o = pl.ds(pl.multiple_of(t * TILE, TILE), TILE)
         got = []
         for half in range(2):
-            value = acc[half, o, :] * lam[o, :]
+            value = acc[half, o, :] * lam[o, :1]
             acc[half, o, :] = value
             got.append(split(value))
         for block in range(2):
@@ -265,7 +273,7 @@
     out.wait()
 
 
-def merge(q_turned, vectors, source, roots, poles, weights, deflated, triangles):
+def merge(q_turned, vectors, order, roots, poles, weights, deflated, triangles):
     depth, width = q_turned.shape[1], q_turned.shape[2]
     size = vectors.shape[3]
     vmem = pl.BlockSpec(memory_space=pltpu.VMEM)
@@ -285,11 +293,14 @@
             pltpu.VMEM((8, 2, 2, depth, width), F32),
             pltpu.VMEM((2, width, width), F32),
             pltpu.VMEM((2, width, width), F32),
-            pltpu.VMEM((width, 1), F32),
-            pltpu.VMEM((width, 1), F32),
-            pltpu.VMEM((width, 1), F32),
-            pltpu.VMEM((TILE, span), BF16),
-            pltpu.VMEM((TILE, span), BF16),
+            pltpu.VMEM((16, span), F32),
+            pltpu.VMEM((16, span), F32),
+            pltpu.VMEM((width, LANES), F32),
+            pltpu.VMEM((width, LANES), F32),
+            pltpu.VMEM((width, LANES), F32),
+            pltpu.VMEM((width, LANES), F32),
+            pltpu.VMEM((width // TILE, TILE, span), BF16),
+            pltpu.VMEM((width // TILE, TILE, span), BF16),
             pltpu.VMEM((span, width), BF16),
             pltpu.VMEM((span, width), BF16),
             pltpu.VMEM((width, 2 * size), F32),
@@ -308,7 +319,7 @@
             collective_id=0, has_side_effects=True, vmem_limit_bytes=60 * 1024 * 1024
         ),
         name="merge",
-    )(q_turned, vectors, source, roots, poles, weights, deflated, triangles)
+    )(q_turned, vectors, order, roots, poles, weights, deflated, triangles)
 
 
 def update_kernel(mixed_ref, vec_ref, high_ref, low_ref, out_ref):
@@ -344,14 +355,11 @@
 def local(
     q_halves, pole_values, weights, secular_roots, column_order, deflated, reflectors, triangles
 ):
-    depth = q_halves.shape[2]
-    col = lax.axis_index("col")
-    source = lax.dynamic_slice_in_dim(column_order, col * 2 * depth, 2 * depth).reshape(-1, 1)
-    lines = (16, 2 * depth)
+    lines = (-1, LANES)
     mixed, high, low = merge(
         jnp.swapaxes(q_halves, 1, 2),
         reflectors,
-        source,
+        column_order.reshape(lines),
         secular_roots.reshape(lines),
         pole_values.reshape(lines),
         weights.reshape(lines),

time: 190 us -> 162 us (0.85)
  Pallas kernels: 178 us -> 158 us
  local copies, waits for them, and re-layouts: 11.5 us -> 4.1 us
    pallas_call x1, Pallas kernels: 173 us -> 153 us  [merge(): pl.pallas_call(merge_kernel, out_shape=(jax.ShapeDtypeStruct((2, width, w...]
    reshape x5 -> x0, local copies, waits for them, and re-layouts: 6.48 us -> none  [the longest x1 1.4 us: local(): pole_values.reshape(lines)]
where the time goes in v2:
time: 162 us
  Pallas kernels  158 us (98%)
  local copies, waits for them, and re-layouts  4.1 us (3%)
    pallas_call x1, Pallas kernels, merge(): pl.pallas_call(merge_kernel, out_shape=(jax.ShapeDtypeStruct((2, width, w...  153 us
    pallas_call x1, Pallas kernels, update(): pl.pallas_call(update_kernel, grid=(2, height // part), out_shape=jax.Sha...  5.02 us
    unnamed x8, local copies, waits for them, and re-layouts  4.1 us

profile of v2, /device:TPU:1, one launch (start us, length us, event | category | flops | bytes accessed | tf_op | source)
XLA Modules:
  0.0 161.8 jit_solution(17300472564240588425)
XLA Ops:
  0.0 0.0 copy-start
  0.0 152.6 %merge.1 = (f32[2,640,640]{2,1,0:T(8,128)}, bf16[640,512]{1,0:T(8,128)(2,1)}, bf16[640,512]{1,0:T(8,128)(2,1)}) custom-call(f32[2,320,640]{2,1,0:T(8,128)} %bitcast.6, f32[2,2,640,256]{3,2,1,0:T(8,128)} %vec_ref.3, s32[80,128]{1,0:T(8,128)} %bitcast.7, f32[80,128]{1,0:T(8,128)} %bitcast.8, f32[80,128]{1,0:T(8,128)} %bitcast.9, f32[80,128]{1,0:T(8,128)} %bitcast.10, ...), custom_call_target="tpu_custom_call" | custom-call | tf_op jit(solution)/shard_map/merge/pallas_call | solution.py:283
  152.6 0.0 copy-done
  152.6 0.0 copy-start.1
  152.6 1.9 %copy-done.1 = f32[2,640,640]{2,1,0:T(8,128)S(1)} copy-done((f32[2,640,640]{2,1,0:T(8,128)S(1)}, f32[2,640,640]{2,1,0:T(8,128)}, u32[]{:S(2)}) %copy-start.1) | copy-done | bytes 3276824
  154.6 0.0 copy-start.2
  154.6 1.1 copy-done.2
  155.7 0.0 copy-start.3
  155.7 1.1 copy-done.3
  156.7 5.0 %update.1 = f32[2,640,640]{2,1,0:T(8,128)} custom-call(f32[2,640,640]{2,1,0:T(8,128)S(1)} %copy-done.1, f32[2,2,640,256]{3,2,1,0:T(8,128)S(1)} %copy-done, bf16[640,512]{1,0:T(8,128)(2,1)S(1)} %copy-done.2, bf16[640,512]{1,0:T(8,128)(2,1)S(1)} %copy-done.3), custom_call_target="tpu_custom_call" | custom-call | tf_op jit(solution)/shard_map/update/pallas_call | solution.py:339
Async XLA Ops:
  0.0 152.6 %copy-start = (f32[2,2,640,256]{3,2,1,0:T(8,128)S(1)}, f32[2,2,640,256]{3,2,1,0:T(8,128)}, u32[]{:S(2)}) copy-start(f32[2,2,640,256]{3,2,1,0:T(8,128)} %vec_ref.3) | copy-start | bytes 7864324
  152.6 1.9 %copy-start.1 = (f32[2,640,640]{2,1,0:T(8,128)S(1)}, f32[2,640,640]{2,1,0:T(8,128)}, u32[]{:S(2)}) copy-start(f32[2,640,640]{2,1,0:T(8,128)} %get-tuple-element.8.mixed_ref) | copy-start | bytes 9830404
  154.6 1.1 copy-start.2
  155.7 1.1 copy-start.3

commit v3 on v2

--- a/solution.py
+++ b/solution.py
@@ -29,15 +29,17 @@
 
 def merge_kernel(
     q_ref, vec_ref, order_ref, roots_ref, lines_ref, weights_ref, deflated_ref, tri_ref,
-    mixed_ref, high_ref, low_ref,
-    panel, acc, turned, poles_ref, zeds_ref, source, lam, keep, squares, c_high, c_low, q_high, q_low,
-    proj, proj_in, coef, cross, cross_in, cross_all,
+    turned_ref,
+    panel, acc, poles_ref, zeds_ref, pole_cols, zed_cols, marks, source, lam, keep, squares,
+    c_high, c_low, q_high, q_low, wall, proj, z_in, part, x_in, coef, cross, cross_in, cross_all,
     local_sem, send, recv, row_send, row_recv,
 ):
     r, col = lax.axis_index("row"), lax.axis_index("col")
     y, x, c = col // 4, lax.rem(col // 2, 2), lax.rem(col, 2)
     width = acc.shape[1]
     piece = width // 8
+    z, low = r // 2, lax.rem(r, 2)
+    size = vec_ref.shape[3]
 
     def dev(dy, dx, dc):
         return (r, lax.rem(y + dy, 4) * 4 + lax.rem(x + dx, 2) * 2 + lax.rem(c + dc, 2))
@@ -49,9 +51,9 @@
     rows = [(lax.rem(r + d, 8), col) for d in range(1, 8)]
 
     barrier = pltpu.get_barrier_semaphore()
-    for other in [up, down, over, twin, *rows]:
+    for other in [up, down, dev(2, 0, 0), over, twin, *rows]:
         pl.semaphore_signal(barrier, inc=1, device_id=other, device_id_type=MESH)
-    pl.semaphore_wait(barrier, 11)
+    pl.semaphore_wait(barrier, 12)
 
     started = {}
 
@@ -63,6 +65,7 @@
         )
         copy.start()
         started[name] = copy
+        return copy
 
     def relay(name, dy, dx, half, to):
         place = panel.at[slot(dy, dx), half, c]
@@ -78,6 +81,7 @@
         other = panel.at[slot(0, 0), 1 - half, c]
         ship(("down", 1 - half), q_ref.at[1 - half], other, down)
         ship(("twin", 0, 0, half), q_ref.at[half], place, twin)
+    ship(("over", 0), q_ref.at[0], panel.at[slot(0, 0), 0, c], over)
 
     total = jnp.zeros(cross.shape, F32)
     for half in range(2):
@@ -99,8 +103,40 @@
 
     cross_copies = row_copies(0, lambda to: cross.at[pl.ds(to * small, small)], cross_in.at[r])
 
+    def one_row(at, src, dst, to):
+        copy = pltpu.make_async_remote_copy(
+            src_ref=src, dst_ref=dst, send_sem=row_send.at[at], recv_sem=row_recv.at[at],
+            device_id=(to, col), device_id_type=MESH,
+        )
+        copy.start()
+        return copy
+
+    def scatter_z(base, which):
+        copies = []
+        for d in range(1, 4):
+            to = lax.rem(z + d, 4)
+            src = proj.at[which, pl.ds(to * 2 * piece, 2 * piece)]
+            copies.append(one_row(base + d, src, z_in.at[which, z], to * 2 + low))
+        return copies
+
+    def scatter_x(base, which, copies):
+        for copy in copies:
+            copy.wait()
+        total = proj[which, pl.ds(z * 2 * piece, 2 * piece), :]
+        for d in range(1, 4):
+            total += z_in[which, lax.rem(z + d, 4)]
+        part[which] = total
+        src = part.at[which, pl.ds((1 - low) * piece, piece)]
+        return one_row(base, src, x_in.at[which], z * 2 + 1 - low)
+
+    depth = panel.shape[3]
     for half in range(2):
-        ship(("over", half), q_ref.at[half], panel.at[slot(0, 0), half, c], over)
+        own[half].wait()
+        got = split(panel[slot(0, 0), half, c])
+        for block in range(2):
+            at = (0, slice(half * depth, (half + 1) * depth), slice(block * size, (block + 1) * size))
+            proj[at] = dot3(got, split(vec_ref[block, half]), (1, 0))
+    w_copies = scatter_z(16, 0)
 
     span = 2 * panel.shape[3]
     group = span // LANES
@@ -138,6 +174,41 @@
         return carry
 
     lax.fori_loop(0, width // STRIP, find, 0)
+
+    w_copy = scatter_x(20, 0, w_copies)
+    ship(("over", 1), q_ref.at[1], panel.at[slot(0, 0), 1, c], over)
+    for i in range(width // LANES):
+        o = slice(i * LANES, (i + 1) * LANES)
+        for line, values in enumerate((lam, keep, source)):
+            marks[line : line + 1, o] = values[o, :].T[:1, :]
+    for i in range(group):
+        o = slice(i * LANES, (i + 1) * LANES)
+        for half in range(2):
+            pole_cols[half, o, :] = poles_ref[half * 8 : (half + 1) * 8, o].T
+            zed_cols[half, o, :] = zeds_ref[half * 8 : (half + 1) * 8, o].T
+
+    def coefficients(core, carry):
+        half, first = r // 4, core * depth + lax.rem(r, 4) * piece
+        lines = pl.ds(pl.multiple_of(first, 16), piece)
+        inner = lax.broadcasted_iota(jnp.int32, (piece, 1), 0)
+        for dx in range(2):
+            for dy in range(4):
+                m = dy * 2 + dx
+                pole = pole_cols[half, lines, m : m + 1]
+                zed = zed_cols[half, lines, m : m + 1]
+                count = (half * 8 * span + m * span + first + inner).astype(F32)
+                into = slice((dx * 4 + dy) * piece, (dx * 4 + dy + 1) * piece)
+                for i in range(width // LANES):
+                    o = slice(i * LANES, (i + 1) * LANES)
+                    gap = pole - marks[0:1, o]
+                    guess = pl.reciprocal(gap, approx=True)
+                    guess = guess * (2.0 - gap * guess)
+                    value = zed * guess * marks[1:2, o]
+                    value = jnp.where(marks[2:3, o] == count, 1.0, value)
+                    q_high[into, o], q_low[into, o] = split(value)
+        w = split(wall[core].reshape(8 * piece, 2 * size))
+        proj[1] += dot3((q_high[...], q_low[...]), w, (0, 0))
+        return carry
 
     def unit(m, half):
         at = half * 8 + m
@@ -180,10 +251,14 @@
         for dy, dx, half in places:
             started["twin", dy, dx, half].wait_recv()
 
-    for half in range(2):
-        own[half].wait()
     ready((0, 0, 0), (0, 0, 1))
     run(2, lambda i: (0, 0, i))
+
+    w_copy.wait()
+    spot = wall.at[c, x, y]
+    wall[c, x, y] = part[0, pl.ds(low * piece, piece), :] + x_in[0]
+    for d in range(1, 4):
+        ship(("w", d), spot, spot, dev(d, 0, 0))
 
     arrive(("up", 0), 3, 0, 0)
     relay(("up2", 0), 3, 0, 0, up)
@@ -206,71 +281,84 @@
 
     arrive(("up", 1), 3, 0, 1)
     arrive(("down", 0), 1, 0, 0)
+    for d in range(1, 4):
+        started["w", d].wait_recv()
+    ship("wx", wall.at[c, x], wall.at[c, x], over)
     arrive(("over", 1), 0, 1, 1)
     relay(("upx", 1), 0, 1, 1, up)
     relay(("downx", 1), 0, 1, 1, down)
     ready((3, 0, 1), (1, 0, 0), (0, 1, 1))
     run(3, lambda i: (3 - 2 * i + i // 2, i // 2, 1 - lax.rem(i, 2)))
 
+    started["wx"].wait_recv()
+    ship("wtwin", wall.at[c], wall.at[c], twin)
     arrive(("up2", 0), 2, 0, 0)
     relay(("over2", 0), 2, 0, 0, over)
     arrive(("down2", 1), 2, 0, 1)
-    relay(("over2", 1), 2, 0, 1, over)
+    started["wtwin"].wait_recv()
+    proj[1] = jnp.zeros(proj.shape[1:], F32)
+    lax.fori_loop(0, 2, coefficients, 0)
+    z_copies = scatter_z(24, 1)
     ready((2, 0, 0), (2, 0, 1))
     run(2, lambda i: (2, 0, i))
-
-    for half in range(2):
-        arrive(("upx", half), 3, 1, half)
-        arrive(("downx", half), 1, 1, half)
-        arrive(("over2", half), 2, 1, half)
-        ready((3, 1, half), (1, 1, half), (2, 1, half))
-        run(3, lambda i, half=half: (3 - 2 * i + 3 * (i // 2), 1, half))
-
-    size = vec_ref.shape[3]
-    norm = lax.rsqrt(jnp.sum(squares[...], axis=1, keepdims=True) + EPSILON)
-    lam[...] = jnp.where(keep[...] > 0, norm, 1.0)
-
-    def project(t, carry):
-        o = pl.ds(pl.multiple_of(t * TILE, TILE), TILE)
-        got = []
-        for half in range(2):
-            value = acc[half, o, :] * lam[o, :1]
-            acc[half, o, :] = value
-            got.append(split(value))
-        for block in range(2):
-            proj[o, block * size : (block + 1) * size] = dot3(
-                got[0], split(vec_ref[block, 0]), (1, 0)
-            ) + dot3(got[1], split(vec_ref[block, 1]), (1, 0))
-        return carry
-
-    lax.fori_loop(0, width // TILE, project, 0)
-    proj_copies = row_copies(16, lambda to: proj.at[pl.ds(to * piece, piece)], proj_in.at[r])
-
-    for half in range(2):
-        turned[half] = acc[half].T
-    out = pltpu.make_async_copy(turned, mixed_ref, local_sem.at[2])
-    out.start()
+    z_copy = scatter_x(28, 1, z_copies)
+    relay(("over2", 1), 2, 0, 1, over)
+
+    arrive(("upx", 0), 3, 1, 0)
+    arrive(("downx", 0), 1, 1, 0)
+    ready((3, 1, 0), (1, 1, 0))
+    run(1, lambda i: (3, 1, 0))
 
     for copy in cross_copies:
         copy.wait()
-    for copy in proj_copies:
-        copy.wait()
+    z_copy.wait()
     mine = pl.ds(r * piece, piece)
-    total = proj[mine, :]
-    for d in range(1, 8):
-        total += proj_in[lax.rem(r + d, 8)]
+    total = part[1, pl.ds(low * piece, piece), :] + x_in[1]
     order = [lax.broadcasted_iota(jnp.int32, (size, size), i) for i in range(2)]
     upper = [split(jnp.where(order[0] <= order[1], tri_ref[i], 0.0)) for i in range(2)]
     second = dot3(split(total[:, size:]), upper[1], (1, 1))
     rest = total[:, :size] - dot3(split(second), split(cross_all[...]), (1, 1))
     coef[mine, :size] = dot3(split(rest), upper[0], (1, 1))
     coef[mine, size:] = second
-    for copy in row_copies(24, lambda to: coef.at[mine], coef.at[mine]):
+    to_x = one_row(29, coef.at[mine], coef.at[mine], z * 2 + 1 - low)
+    run(1, lambda i: (1, 1, 0))
+    to_x.wait()
+    mine = pl.ds(z * 2 * piece, 2 * piece)
+    to_z = []
+    for d in range(1, 4):
+        to = lax.rem(z + d, 4)
+        to_z.append(one_row(29 + d, coef.at[mine], coef.at[mine], to * 2 + low))
+    arrive(("over2", 0), 2, 1, 0)
+    ready((2, 1, 0))
+    run(1, lambda i: (2, 1, 0))
+
+    arrive(("upx", 1), 3, 1, 1)
+    arrive(("downx", 1), 1, 1, 1)
+    arrive(("over2", 1), 2, 1, 1)
+    ready((3, 1, 1), (1, 1, 1), (2, 1, 1))
+    run(3, lambda i: (3 - 2 * i + 3 * (i // 2), 1, 1))
+
+    for copy in to_z:
         copy.wait()
-    high_ref[...], low_ref[...] = split(coef[...])
+    norm = lax.rsqrt(jnp.sum(squares[...], axis=1, keepdims=True) + EPSILON)
+    lam[...] = jnp.where(keep[...] > 0, norm, 1.0)
+    out = []
+    for half in range(2):
+        sides = [split(vec_ref[block, half]) for block in range(2)]
+        for t in range(width // TILE):
+            o = slice(t * TILE, (t + 1) * TILE)
+            value = acc[half, o, :]
+            for block in range(2):
+                some = split(coef[o, block * size : (block + 1) * size])
+                value -= dot3(some, sides[block], (1, 1))
+            acc[half, o, :] = value * lam[o, :1]
+        copy = pltpu.make_async_copy(acc.at[half], turned_ref.at[half], local_sem.at[half])
+        copy.start()
+        out.append(copy)
     for copy in started.values():
         copy.wait_send()
-    out.wait()
+    for copy in out:
+        copy.wait()
 
 
 def merge(q_turned, vectors, order, roots, poles, weights, deflated, triangles):
@@ -279,42 +367,40 @@
     vmem = pl.BlockSpec(memory_space=pltpu.VMEM)
     hbm = pl.BlockSpec(memory_space=pl.ANY)
     dma = pltpu.SemaphoreType.DMA
-    span = 2 * depth
+    span, piece = 2 * depth, width // 8
+    scratch = [
+        ((8, 2, 2, depth, width), F32),
+        ((2, width, width), F32),
+        ((16, span), F32),
+        ((16, span), F32),
+        ((2, span, 8), F32),
+        ((2, span, 8), F32),
+        ((8, width), F32),
+        ((width, LANES), F32),
+        ((width, LANES), F32),
+        ((width, LANES), F32),
+        ((width, LANES), F32),
+        ((width // TILE, TILE, span), BF16),
+        ((width // TILE, TILE, span), BF16),
+        ((span, width), BF16),
+        ((span, width), BF16),
+        ((2, 2, 4, piece, 2 * size), F32),
+        ((2, width, 2 * size), F32),
+        ((2, 4, 2 * piece, 2 * size), F32),
+        ((2, 2 * piece, 2 * size), F32),
+        ((2, piece, 2 * size), F32),
+        ((width, 2 * size), F32),
+        ((size, size), F32),
+        ((8, size // 8, size), F32),
+        ((size, size), F32),
+    ]
     return pl.pallas_call(
         merge_kernel,
-        out_shape=(
-            jax.ShapeDtypeStruct((2, width, width), F32),
-            jax.ShapeDtypeStruct((width, 2 * size), BF16),
-            jax.ShapeDtypeStruct((width, 2 * size), BF16),
-        ),
+        out_shape=jax.ShapeDtypeStruct((2, width, width), F32),
         in_specs=[hbm] + [vmem] * 7,
-        out_specs=(hbm, vmem, vmem),
-        scratch_shapes=[
-            pltpu.VMEM((8, 2, 2, depth, width), F32),
-            pltpu.VMEM((2, width, width), F32),
-            pltpu.VMEM((2, width, width), F32),
-            pltpu.VMEM((16, span), F32),
-            pltpu.VMEM((16, span), F32),
-            pltpu.VMEM((width, LANES), F32),
-            pltpu.VMEM((width, LANES), F32),
-            pltpu.VMEM((width, LANES), F32),
-            pltpu.VMEM((width, LANES), F32),
-            pltpu.VMEM((width // TILE, TILE, span), BF16),
-            pltpu.VMEM((width // TILE, TILE, span), BF16),
-            pltpu.VMEM((span, width), BF16),
-            pltpu.VMEM((span, width), BF16),
-            pltpu.VMEM((width, 2 * size), F32),
-            pltpu.VMEM((8, width // 8, 2 * size), F32),
-            pltpu.VMEM((width, 2 * size), F32),
-            pltpu.VMEM((size, size), F32),
-            pltpu.VMEM((8, size // 8, size), F32),
-            pltpu.VMEM((size, size), F32),
-            dma((3,)),
-            dma((32,)),
-            dma((32,)),
-            dma((32,)),
-            dma((32,)),
-        ],
+        out_specs=hbm,
+        scratch_shapes=[pltpu.VMEM(*one) for one in scratch]
+        + [dma((2,)), dma((40,)), dma((40,)), dma((40,)), dma((40,))],
         compiler_params=pltpu.CompilerParams(
             collective_id=0, has_side_effects=True, vmem_limit_bytes=60 * 1024 * 1024
         ),
@@ -322,41 +408,28 @@
     )(q_turned, vectors, order, roots, poles, weights, deflated, triangles)
 
 
-def update_kernel(mixed_ref, vec_ref, high_ref, low_ref, out_ref):
-    size = vec_ref.shape[3]
-    total = mixed_ref[0]
-    for block in range(2):
-        take = slice(block * size, (block + 1) * size)
-        total -= dot3(split(vec_ref[block, 0]), (high_ref[:, take], low_ref[:, take]), (1, 1))
-    out_ref[0] = total
-
-
-def update(mixed, vectors, high, low):
-    _, height, width = mixed.shape
-    size = vectors.shape[3]
-    part = 320
-    whole = pl.BlockSpec((width, 2 * size), lambda h, i: (0, 0))
+def turn_kernel(turned_ref, out_ref):
+    out_ref[0] = turned_ref[0].T
+
+
+def turn(turned):
+    _, width, height = turned.shape
     return pl.pallas_call(
-        update_kernel,
-        grid=(2, height // part),
-        out_shape=jax.ShapeDtypeStruct(mixed.shape, F32),
-        in_specs=[
-            pl.BlockSpec((1, part, width), lambda h, i: (h, i, 0)),
-            pl.BlockSpec((2, 1, part, size), lambda h, i: (0, h, i, 0)),
-            whole,
-            whole,
-        ],
-        out_specs=pl.BlockSpec((1, part, width), lambda h, i: (h, i, 0)),
-        compiler_params=pltpu.CompilerParams(vmem_limit_bytes=32 * 1024 * 1024),
-        name="update",
-    )(mixed, vectors, high, low)
+        turn_kernel,
+        grid=(2, height // LANES),
+        out_shape=jax.ShapeDtypeStruct((2, height, width), F32),
+        in_specs=[pl.BlockSpec((1, width, LANES), lambda h, i: (h, 0, i))],
+        out_specs=pl.BlockSpec((1, LANES, width), lambda h, i: (h, i, 0)),
+        compiler_params=pltpu.CompilerParams(vmem_limit_bytes=60 * 1024 * 1024),
+        name="turn",
+    )(turned)
 
 
 def local(
     q_halves, pole_values, weights, secular_roots, column_order, deflated, reflectors, triangles
 ):
     lines = (-1, LANES)
-    mixed, high, low = merge(
+    turned = merge(
         jnp.swapaxes(q_halves, 1, 2),
         reflectors,
         column_order.reshape(lines),
@@ -366,7 +439,7 @@
         deflated.reshape(lines),
         triangles,
     )
-    return update(mixed, reflectors, high, low)
+    return turn(turned)
 
 
 def solution(mesh):

time: 162 us -> 153 us (0.944)
  Pallas kernels: 158 us -> 153 us
  local copies, waits for them, and re-layouts: 4.1 us -> 0 us
    pallas_call x2, Pallas kernels: 158 us -> 153 us  [the longest x1 145 us: merge(): pl.pallas_call(merge_kernel, out_shape=jax.ShapeDtypeStruct((2, width, wi...]
    unnamed x8 -> x0, local copies, waits for them, and re-layouts: 4.1 us -> none
where the time goes in v3:
time: 153 us
  Pallas kernels  153 us (100%)
    pallas_call x1, Pallas kernels, merge(): pl.pallas_call(merge_kernel, out_shape=jax.ShapeDtypeStruct((2, width, wi...  145 us
    pallas_call x1, Pallas kernels, turn(): pl.pallas_call(turn_kernel, grid=(2, height // LANES), out_shape=jax.Shap...  7.68 us

profile of v3, /device:TPU:1, one launch (start us, length us, event | category | flops | bytes accessed | tf_op | source)
XLA Modules:
  0.0 152.9 jit_solution(11669706464059233484)
XLA Ops:
  0.0 145.2 %merge.1.turned_ref = f32[2,640,640]{2,1,0:T(8,128)} custom-call(f32[2,320,640]{2,1,0:T(8,128)} %bitcast.6, f32[2,2,640,256]{3,2,1,0:T(8,128)} %vec_ref.1, s32[80,128]{1,0:T(8,128)} %bitcast.7, f32[80,128]{1,0:T(8,128)} %bitcast.8, f32[80,128]{1,0:T(8,128)} %bitcast.9, f32[80,128]{1,0:T(8,128)} %bitcast.10, s32[80,128]{1,0:T(8,128)} %bitcast.11, ...), custom_call_target="tpu_custom_call" | custom-call | tf_op jit(solution)/shard_map/merge/pallas_call | solution.py:397
  145.2 7.7 %turn.1 = f32[2,640,640]{2,1,0:T(8,128)} custom-call(f32[2,640,640]{2,1,0:T(8,128)} %merge.1.turned_ref), custom_call_target="tpu_custom_call" | custom-call | tf_op jit(solution)/shard_map/turn/pallas_call | solution.py:417

commit v4 on v3

--- a/solution.py
+++ b/solution.py
@@ -71,23 +71,29 @@
         place = panel.at[slot(dy, dx), half, c]
         ship(name, place, place, to)
 
+    def ship_part(name, half, part_of, to):
+        lines = pl.ds(part_of * (depth // 2), depth // 2)
+        ship((name, part_of), q_ref.at[half, lines], panel.at[slot(0, 0), half, c, lines], to)
+
+    def relay_part(name, dy, dx, half, part_of, to):
+        lines = pl.ds(part_of * (depth // 2), depth // 2)
+        place = panel.at[slot(dy, dx), half, c, lines]
+        ship(name, place, place, to)
+
     own = []
+    depth = panel.shape[3]
     for half in range(2):
         place = panel.at[slot(0, 0), half, c]
         mine = pltpu.make_async_copy(q_ref.at[half], place, local_sem.at[half])
         mine.start()
         own.append(mine)
-        ship(("up", half), q_ref.at[half], place, up)
-        other = panel.at[slot(0, 0), 1 - half, c]
-        ship(("down", 1 - half), q_ref.at[1 - half], other, down)
-        ship(("twin", 0, 0, half), q_ref.at[half], place, twin)
-    ship(("over", 0), q_ref.at[0], panel.at[slot(0, 0), 0, c], over)
-
-    total = jnp.zeros(cross.shape, F32)
+    for name, half, to in (("up", 0, up), ("down", 1, down), ("over", 0, over)):
+        ship((name, half), q_ref.at[half], panel.at[slot(0, 0), half, c], to)
     for half in range(2):
-        total += dot3(split(vec_ref[0, half]), split(vec_ref[1, half]), (0, 0))
-    cross[...] = total
-    small = cross.shape[0] // 8
+        ship(("twin", 0, 0, half), q_ref.at[half], panel.at[slot(0, 0), half, c], twin)
+    for part_of in range(2):
+        ship_part("up1", 1, part_of, up)
+        ship_part("down0", 0, part_of, down)
 
     def row_copies(base, src_of, dst):
         copies = []
@@ -101,8 +107,6 @@
             copies.append(copy)
         return copies
 
-    cross_copies = row_copies(0, lambda to: cross.at[pl.ds(to * small, small)], cross_in.at[r])
-
     def one_row(at, src, dst, to):
         copy = pltpu.make_async_remote_copy(
             src_ref=src, dst_ref=dst, send_sem=row_send.at[at], recv_sem=row_recv.at[at],
@@ -129,7 +133,6 @@
         src = part.at[which, pl.ds((1 - low) * piece, piece)]
         return one_row(base, src, x_in.at[which], z * 2 + 1 - low)
 
-    depth = panel.shape[3]
     for half in range(2):
         own[half].wait()
         got = split(panel[slot(0, 0), half, c])
@@ -137,6 +140,7 @@
             at = (0, slice(half * depth, (half + 1) * depth), slice(block * size, (block + 1) * size))
             proj[at] = dot3(got, split(vec_ref[block, half]), (1, 0))
     w_copies = scatter_z(16, 0)
+
 
     span = 2 * panel.shape[3]
     group = span // LANES
@@ -176,7 +180,8 @@
     lax.fori_loop(0, width // STRIP, find, 0)
 
     w_copy = scatter_x(20, 0, w_copies)
-    ship(("over", 1), q_ref.at[1], panel.at[slot(0, 0), 1, c], over)
+    for part_of in range(2):
+        ship_part("over1", 1, part_of, over)
     for i in range(width // LANES):
         o = slice(i * LANES, (i + 1) * LANES)
         for line, values in enumerate((lam, keep, source)):
@@ -270,6 +275,31 @@
     ready((3, 0, 0), (1, 0, 1), (0, 1, 0))
     run(3, lambda i: (3 - 2 * i + i // 2, i // 2, lax.rem(i, 2)))
 
+    total = jnp.zeros(cross.shape, F32)
+    for half in range(2):
+        total += dot3(split(vec_ref[0, half]), split(vec_ref[1, half]), (0, 0))
+    cross[...] = total
+
+    small = cross.shape[0] // 8
+    cross_copies = row_copies(0, lambda to: cross.at[pl.ds(to * small, small)], cross_in.at[r])
+
+    started["up1", 0].wait_recv()
+    arrive(("up1", 1), 3, 0, 1)
+    started["down0", 0].wait_recv()
+    arrive(("down0", 1), 1, 0, 0)
+    ready((3, 0, 1), (1, 0, 0))
+    run(2, lambda i: (3 - 2 * i, 0, 1 - i))
+    for d in range(1, 4):
+        started["w", d].wait_recv()
+    ship("wx", wall.at[c, x], wall.at[c, x], over)
+
+    started["over1", 0].wait_recv()
+    arrive(("over1", 1), 0, 1, 1)
+    relay(("upx", 1), 0, 1, 1, up)
+    relay(("downx", 1), 0, 1, 1, down)
+    ready((0, 1, 1))
+    run(1, lambda i: (0, 1, 1))
+
     for copy in cross_copies:
         copy.wait()
     mine = pl.ds(r * small, small)
@@ -279,35 +309,23 @@
     cross_all[mine, :] = total
     cross_copies = row_copies(8, lambda to: cross_all.at[mine], cross_all.at[mine])
 
-    arrive(("up", 1), 3, 0, 1)
-    arrive(("down", 0), 1, 0, 0)
-    for d in range(1, 4):
-        started["w", d].wait_recv()
-    ship("wx", wall.at[c, x], wall.at[c, x], over)
-    arrive(("over", 1), 0, 1, 1)
-    relay(("upx", 1), 0, 1, 1, up)
-    relay(("downx", 1), 0, 1, 1, down)
-    ready((3, 0, 1), (1, 0, 0), (0, 1, 1))
-    run(3, lambda i: (3 - 2 * i + i // 2, i // 2, 1 - lax.rem(i, 2)))
-
     started["wx"].wait_recv()
     ship("wtwin", wall.at[c], wall.at[c], twin)
     arrive(("up2", 0), 2, 0, 0)
     relay(("over2", 0), 2, 0, 0, over)
     arrive(("down2", 1), 2, 0, 1)
+    proj[1] = jnp.zeros(proj.shape[1:], F32)
     started["wtwin"].wait_recv()
-    proj[1] = jnp.zeros(proj.shape[1:], F32)
     lax.fori_loop(0, 2, coefficients, 0)
     z_copies = scatter_z(24, 1)
     ready((2, 0, 0), (2, 0, 1))
     run(2, lambda i: (2, 0, i))
     z_copy = scatter_x(28, 1, z_copies)
-    relay(("over2", 1), 2, 0, 1, over)
 
     arrive(("upx", 0), 3, 1, 0)
     arrive(("downx", 0), 1, 1, 0)
     ready((3, 1, 0), (1, 1, 0))
-    run(1, lambda i: (3, 1, 0))
+    run(2, lambda i: (3 - 2 * i, 1, 0))
 
     for copy in cross_copies:
         copy.wait()
@@ -321,22 +339,26 @@
     coef[mine, :size] = dot3(split(rest), upper[0], (1, 1))
     coef[mine, size:] = second
     to_x = one_row(29, coef.at[mine], coef.at[mine], z * 2 + 1 - low)
-    run(1, lambda i: (1, 1, 0))
+    arrive(("over2", 0), 2, 1, 0)
     to_x.wait()
     mine = pl.ds(z * 2 * piece, 2 * piece)
     to_z = []
     for d in range(1, 4):
         to = lax.rem(z + d, 4)
         to_z.append(one_row(29 + d, coef.at[mine], coef.at[mine], to * 2 + low))
-    arrive(("over2", 0), 2, 1, 0)
     ready((2, 1, 0))
     run(1, lambda i: (2, 1, 0))
 
     arrive(("upx", 1), 3, 1, 1)
+    relay_part("up3", 3, 1, 1, 0, up)
     arrive(("downx", 1), 1, 1, 1)
-    arrive(("over2", 1), 2, 1, 1)
-    ready((3, 1, 1), (1, 1, 1), (2, 1, 1))
-    run(3, lambda i: (3 - 2 * i + 3 * (i // 2), 1, 1))
+    relay_part("down3", 1, 1, 1, 1, down)
+    ready((3, 1, 1), (1, 1, 1))
+    run(2, lambda i: (3 - 2 * i, 1, 1))
+    started["up3"].wait_recv()
+    arrive("down3", 2, 1, 1)
+    ready((2, 1, 1))
+    run(1, lambda i: (2, 1, 1))
 
     for copy in to_z:
         copy.wait()
@@ -416,10 +438,10 @@
     _, width, height = turned.shape
     return pl.pallas_call(
         turn_kernel,
-        grid=(2, height // LANES),
+        grid=(2,),
         out_shape=jax.ShapeDtypeStruct((2, height, width), F32),
-        in_specs=[pl.BlockSpec((1, width, LANES), lambda h, i: (h, 0, i))],
-        out_specs=pl.BlockSpec((1, LANES, width), lambda h, i: (h, i, 0)),
+        in_specs=[pl.BlockSpec((1, width, height), lambda h: (h, 0, 0))],
+        out_specs=pl.BlockSpec((1, height, width), lambda h: (h, 0, 0)),
         compiler_params=pltpu.CompilerParams(vmem_limit_bytes=60 * 1024 * 1024),
         name="turn",
     )(turned)

time: 153 us -> 146 us (0.954)
  Pallas kernels: 153 us -> 146 us
    pallas_call x1, Pallas kernels: 7.68 us -> 3.65 us  [turn(): pl.pallas_call(turn_kernel, grid=(2,), out_shape=jax.ShapeDtypeStruct((2,...]
    pallas_call x1, Pallas kernels: 145 us -> 142 us  [merge(): pl.pallas_call(merge_kernel, out_shape=jax.ShapeDtypeStruct((2, width, wi...]
where the time goes in v4:
time: 146 us
  Pallas kernels  146 us (100%)
    pallas_call x1, Pallas kernels, merge(): pl.pallas_call(merge_kernel, out_shape=jax.ShapeDtypeStruct((2, width, wi...  142 us
    pallas_call x1, Pallas kernels, turn(): pl.pallas_call(turn_kernel, grid=(2,), out_shape=jax.ShapeDtypeStruct((2,...  3.65 us

profile of v4, /device:TPU:1, one launch (start us, length us, event | category | flops | bytes accessed | tf_op | source)
XLA Modules:
  0.0 145.7 jit_solution(3850552378268003912)
XLA Ops:
  0.0 142.0 %merge.1.turned_ref = f32[2,640,640]{2,1,0:T(8,128)} custom-call(f32[2,320,640]{2,1,0:T(8,128)} %bitcast.6, f32[2,2,640,256]{3,2,1,0:T(8,128)} %vec_ref.1, s32[80,128]{1,0:T(8,128)} %bitcast.7, f32[80,128]{1,0:T(8,128)} %bitcast.8, f32[80,128]{1,0:T(8,128)} %bitcast.9, f32[80,128]{1,0:T(8,128)} %bitcast.10, s32[80,128]{1,0:T(8,128)} %bitcast.11, ...), custom_call_target="tpu_custom_call" | custom-call | tf_op jit(solution)/shard_map/merge/pallas_call | solution.py:419
  142.0 3.6 %turn.1 = f32[2,640,640]{2,1,0:T(8,128)} custom-call(f32[2,640,640]{2,1,0:T(8,128)} %merge.1.turned_ref), custom_call_target="tpu_custom_call" | custom-call | tf_op jit(solution)/shard_map/turn/pallas_call | solution.py:439

commit v5 on v4

--- a/solution.py
+++ b/solution.py
@@ -338,14 +338,8 @@
     rest = total[:, :size] - dot3(split(second), split(cross_all[...]), (1, 1))
     coef[mine, :size] = dot3(split(rest), upper[0], (1, 1))
     coef[mine, size:] = second
-    to_x = one_row(29, coef.at[mine], coef.at[mine], z * 2 + 1 - low)
+    share_copies = row_copies(32, lambda to: coef.at[mine], coef.at[mine])
     arrive(("over2", 0), 2, 1, 0)
-    to_x.wait()
-    mine = pl.ds(z * 2 * piece, 2 * piece)
-    to_z = []
-    for d in range(1, 4):
-        to = lax.rem(z + d, 4)
-        to_z.append(one_row(29 + d, coef.at[mine], coef.at[mine], to * 2 + low))
     ready((2, 1, 0))
     run(1, lambda i: (2, 1, 0))
 
@@ -360,7 +354,7 @@
     ready((2, 1, 1))
     run(1, lambda i: (2, 1, 1))
 
-    for copy in to_z:
+    for copy in share_copies:
         copy.wait()
     norm = lax.rsqrt(jnp.sum(squares[...], axis=1, keepdims=True) + EPSILON)
     lam[...] = jnp.where(keep[...] > 0, norm, 1.0)

time: 146 us -> 143 us (0.979)
  Pallas kernels: 146 us -> 142 us
    pallas_call x1, Pallas kernels: 142 us -> 139 us  [merge(): pl.pallas_call(merge_kernel, out_shape=jax.ShapeDtypeStruct((2, width, wi...]
where the time goes in v5:
time: 143 us; the launch traced here: 142 us
  Pallas kernels  142 us (99%)
    pallas_call x1, Pallas kernels, merge(): pl.pallas_call(merge_kernel, out_shape=jax.ShapeDtypeStruct((2, width, wi...  139 us
    pallas_call x1, Pallas kernels, turn(): pl.pallas_call(turn_kernel, grid=(2,), out_shape=jax.ShapeDtypeStruct((2,...  3.65 us

profile of v5, /device:TPU:1, one launch (start us, length us, event | category | flops | bytes accessed | tf_op | source)
XLA Modules:
  0.0 142.4 jit_solution(9813474709160637121)
XLA Ops:
  0.0 138.7 %merge.1.turned_ref = f32[2,640,640]{2,1,0:T(8,128)} custom-call(f32[2,320,640]{2,1,0:T(8,128)} %bitcast.6, f32[2,2,640,256]{3,2,1,0:T(8,128)} %vec_ref.1, s32[80,128]{1,0:T(8,128)} %bitcast.7, f32[80,128]{1,0:T(8,128)} %bitcast.8, f32[80,128]{1,0:T(8,128)} %bitcast.9, f32[80,128]{1,0:T(8,128)} %bitcast.10, s32[80,128]{1,0:T(8,128)} %bitcast.11, ...), custom_call_target="tpu_custom_call" | custom-call | tf_op jit(solution)/shard_map/merge/pallas_call | solution.py:413
  138.7 3.6 %turn.1 = f32[2,640,640]{2,1,0:T(8,128)} custom-call(f32[2,640,640]{2,1,0:T(8,128)} %merge.1.turned_ref), custom_call_target="tpu_custom_call" | custom-call | tf_op jit(solution)/shard_map/turn/pallas_call | solution.py:433

commit v6 on v5

--- a/solution.py
+++ b/solution.py
@@ -317,10 +317,11 @@
     proj[1] = jnp.zeros(proj.shape[1:], F32)
     started["wtwin"].wait_recv()
     lax.fori_loop(0, 2, coefficients, 0)
-    z_copies = scatter_z(24, 1)
+    z_copies = row_copies(
+        24, lambda to: proj.at[1, pl.ds(to * piece, piece)], z_in.at[1, z, pl.ds(low * piece, piece)]
+    )
     ready((2, 0, 0), (2, 0, 1))
     run(2, lambda i: (2, 0, i))
-    z_copy = scatter_x(28, 1, z_copies)
 
     arrive(("upx", 0), 3, 1, 0)
     arrive(("downx", 0), 1, 1, 0)
@@ -329,9 +330,13 @@
 
     for copy in cross_copies:
         copy.wait()
-    z_copy.wait()
+    for copy in z_copies:
+        copy.wait()
     mine = pl.ds(r * piece, piece)
-    total = part[1, pl.ds(low * piece, piece), :] + x_in[1]
+    total = proj[1, mine, :]
+    for d in range(1, 8):
+        other = lax.rem(r + d, 8)
+        total += z_in[1, other // 2, pl.ds(lax.rem(other, 2) * piece, piece), :]
     order = [lax.broadcasted_iota(jnp.int32, (size, size), i) for i in range(2)]
     upper = [split(jnp.where(order[0] <= order[1], tri_ref[i], 0.0)) for i in range(2)]
     second = dot3(split(total[:, size:]), upper[1], (1, 1))

time: 143 us -> 140 us (0.979); the launches traced: 142 us -> 138 us
  Pallas kernels: 142 us -> 138 us
    pallas_call x1, Pallas kernels: 139 us -> 134 us  [merge(): pl.pallas_call(merge_kernel, out_shape=jax.ShapeDtypeStruct((2, width, wi...]
where the time goes in v6:
time: 140 us; the launch traced here: 138 us
  Pallas kernels  138 us (99%)
    pallas_call x1, Pallas kernels, merge(): pl.pallas_call(merge_kernel, out_shape=jax.ShapeDtypeStruct((2, width, wi...  134 us
    pallas_call x1, Pallas kernels, turn(): pl.pallas_call(turn_kernel, grid=(2,), out_shape=jax.ShapeDtypeStruct((2,...  3.65 us

profile of v6, /device:TPU:1, one launch (start us, length us, event | category | flops | bytes accessed | tf_op | source)
XLA Modules:
  0.0 137.8 jit_solution(10198526282950982628)
XLA Ops:
  0.0 134.1 %merge.1.turned_ref = f32[2,640,640]{2,1,0:T(8,128)} custom-call(f32[2,320,640]{2,1,0:T(8,128)} %bitcast.6, f32[2,2,640,256]{3,2,1,0:T(8,128)} %vec_ref.1, s32[80,128]{1,0:T(8,128)} %bitcast.7, f32[80,128]{1,0:T(8,128)} %bitcast.8, f32[80,128]{1,0:T(8,128)} %bitcast.9, f32[80,128]{1,0:T(8,128)} %bitcast.10, s32[80,128]{1,0:T(8,128)} %bitcast.11, ...), custom_call_target="tpu_custom_call" | custom-call | tf_op jit(solution)/shard_map/merge/pallas_call | solution.py:418
  134.1 3.6 %turn.1 = f32[2,640,640]{2,1,0:T(8,128)} custom-call(f32[2,640,640]{2,1,0:T(8,128)} %merge.1.turned_ref), custom_call_target="tpu_custom_call" | custom-call | tf_op jit(solution)/shard_map/turn/pallas_call | solution.py:438

commit v7 on v6

--- a/solution.py
+++ b/solution.py
@@ -311,15 +311,15 @@
 
     started["wx"].wait_recv()
     ship("wtwin", wall.at[c], wall.at[c], twin)
-    arrive(("up2", 0), 2, 0, 0)
-    relay(("over2", 0), 2, 0, 0, over)
-    arrive(("down2", 1), 2, 0, 1)
     proj[1] = jnp.zeros(proj.shape[1:], F32)
     started["wtwin"].wait_recv()
     lax.fori_loop(0, 2, coefficients, 0)
     z_copies = row_copies(
         24, lambda to: proj.at[1, pl.ds(to * piece, piece)], z_in.at[1, z, pl.ds(low * piece, piece)]
     )
+    arrive(("up2", 0), 2, 0, 0)
+    relay(("over2", 0), 2, 0, 0, over)
+    arrive(("down2", 1), 2, 0, 1)
     ready((2, 0, 0), (2, 0, 1))
     run(2, lambda i: (2, 0, i))
 

time: 140 us -> 147 us (1.050); the launches traced: 138 us -> 147 us
  Pallas kernels: 138 us -> 147 us
    pallas_call x1, Pallas kernels: 134 us -> 144 us  [merge(): pl.pallas_call(merge_kernel, out_shape=jax.ShapeDtypeStruct((2, width, wi...]
where the time goes in v7:
time: 147 us
  Pallas kernels  147 us (100%)
    pallas_call x1, Pallas kernels, merge(): pl.pallas_call(merge_kernel, out_shape=jax.ShapeDtypeStruct((2, width, wi...  144 us
    pallas_call x1, Pallas kernels, turn(): pl.pallas_call(turn_kernel, grid=(2,), out_shape=jax.ShapeDtypeStruct((2,...  3.65 us

profile of v7, /device:TPU:1, one launch (start us, length us, event | category | flops | bytes accessed | tf_op | source)
XLA Modules:
  0.0 147.2 jit_solution(8758711057460453901)
XLA Ops:
  0.0 143.6 %merge.1.turned_ref = f32[2,640,640]{2,1,0:T(8,128)} custom-call(f32[2,320,640]{2,1,0:T(8,128)} %bitcast.6, f32[2,2,640,256]{3,2,1,0:T(8,128)} %vec_ref.1, s32[80,128]{1,0:T(8,128)} %bitcast.7, f32[80,128]{1,0:T(8,128)} %bitcast.8, f32[80,128]{1,0:T(8,128)} %bitcast.9, f32[80,128]{1,0:T(8,128)} %bitcast.10, s32[80,128]{1,0:T(8,128)} %bitcast.11, ...), custom_call_target="tpu_custom_call" | custom-call | tf_op jit(solution)/shard_map/merge/pallas_call | solution.py:418
  143.6 3.6 %turn.1 = f32[2,640,640]{2,1,0:T(8,128)} custom-call(f32[2,640,640]{2,1,0:T(8,128)} %merge.1.turned_ref), custom_call_target="tpu_custom_call" | custom-call | tf_op jit(solution)/shard_map/turn/pallas_call | solution.py:438
